TPU v7x, 512 devices: a whole 4x8x8 slice. The times are simulated.
512 devices in a mesh: section: 8 (over x, z_hi), seq: 32 (over z_lo, y), cfg: 2 (over core).
Axes of the slice: x: 4, y: 8, z: 8 (z_hi: 2, z_lo: 4; z = z_hi * 4 + z_lo), core: 2. Of those that a mesh axis runs over, the one named last changes fastest.
Arguments:
- hidden: bfloat16 [2, 8, 1024, 2048], P('cfg', 'section', 'seq'), may hold values from -6 to 6
- queries: bfloat16 [2, 8, 1024, 2048], P('cfg', 'section', 'seq')
- fresh_keys: bfloat16 [2, 8, 1024, 2048], P('cfg', 'section', 'seq'), may hold values from -6 to 6
- fresh_values: bfloat16 [2, 8, 1024, 2048], P('cfg', 'section', 'seq'), may hold values from -6 to 6
- stale_keys: bfloat16 [2, 8, 32, 4224, 128], P('cfg', 'section', 'seq')
- stale_values: bfloat16 [2, 8, 32, 4224, 128], P('cfg', 'section', 'seq'), may hold values from -6 to 6
- gate_table: float32 [50, 8, 2048], P(None, 'section'), may hold values from -6 to 6
- timestep: int32 [], replicated, may hold values from 0 to 49
- patch_index: int32 [], replicated, may hold values from 0 to 7
- text_lengths: int32 [2], P('cfg'), may hold values from 32 to 256, as said below
Outputs:
- handed: bfloat16 [2, 8, 1024, 2048], P('cfg', 'section', 'seq')
Inputs may be any that keep to these rules, and one draw needn't show every extreme that they name: `text_lengths`: one of the two branches has all 256 text tokens live.
All inputs are finite; a program needn't handle non-finite values.
Results may differ from a plain program's by a relative error of at most 0.0075.
Values may be sent and summed in bfloat16 or wider, within the bound.
A program may use at most 64 MiB of HBM per device.

v0:
```python
import jax
import jax.numpy as jnp
from jax import lax
from jax.sharding import PartitionSpec as P

HEADS = 16
PATCHES = 8


GUIDE = 5.0


def passed_along(value, axis, steps):
    count = lax.axis_size(axis)
    pairs = [(source, (source + steps) % count) for source in range(count)]
    return lax.ppermute(value, axis, pairs)


def partner_2(value, axis, distance):
    mask = 2**distance
    pairs = [(source, source ^ mask) for source in range(lax.axis_size(axis))]
    return lax.ppermute(value, axis, pairs)


def stale_mask(key_side, key_half, video_tokens, patch_start, patch_tokens, text_limit):
    positions = key_side * key_half + jnp.arange(key_half, dtype=jnp.int32)
    outside = (positions < patch_start) | (positions >= patch_start + patch_tokens)
    in_text = (positions >= video_tokens) & (positions - video_tokens < text_limit)
    return (positions < video_tokens) & outside | in_text


def partial_attention(query_rows, keys_all, values_all, live, scale):
    row_count = query_rows.shape[0]
    block_rows = row_count
    while block_rows > 512 and block_rows % 2 == 0:
        block_rows = block_rows // 2
    blocks = query_rows.reshape(row_count // block_rows, block_rows, query_rows.shape[1])

    def one_block(query_block):
        scores = (
            lax.dot_general(
                query_block, keys_all, (((1,), (1,)), ((), ())), preferred_element_type=jnp.float32
            )
            * scale
        )
        masked = jnp.where(live[None, :], scores, -jnp.inf)
        highest = jnp.max(masked, axis=1)
        exps = jnp.exp(masked - highest[:, None])
        totals = jnp.sum(exps, axis=1)
        summed = jnp.dot(exps.astype(jnp.bfloat16), values_all, preferred_element_type=jnp.float32)
        return (summed, highest, totals)

    summed, highest, totals = lax.map(one_block, blocks)
    return (summed.reshape(row_count, -1), highest.reshape(row_count), totals.reshape(row_count))


def normalize(summed, highest, totals):
    partial_value = (summed / totals[..., None]).astype(jnp.bfloat16)
    return (partial_value, highest + jnp.log(totals))


def combine_halves(partial_value, lse):
    joint = jnp.max(lse, axis=-1, keepdims=True)
    factor = jnp.exp(lse - joint)
    merged = jnp.sum(partial_value.astype(jnp.float32) * factor[..., None], axis=-2)
    weight = jnp.sum(factor, axis=-1)
    return (merged / weight[..., None]).astype(jnp.bfloat16)


def body(
    hidden,
    queries,
    fresh_keys,
    fresh_values,
    stale_keys,
    stale_values,
    gate_table,
    timestep,
    patch_index,
    text_lengths,
):
    seq_count = lax.axis_size("seq")
    local_tokens = hidden.shape[2]
    features = hidden.shape[3]
    head_dim = features // HEADS
    rows_here = stale_keys.shape[2]
    key_half = stale_keys.shape[3]
    patch_tokens = local_tokens * seq_count
    video_tokens = PATCHES * patch_tokens
    scale = head_dim ** (-0.5)
    section_index = lax.axis_index("section")
    seq_index = lax.axis_index("seq")
    patch_start = jnp.mod(patch_index - section_index, PATCHES) * patch_tokens
    text_limit = text_lengths[0]
    query_local = queries.reshape(local_tokens, HEADS, 1, head_dim)
    query_both = jnp.broadcast_to(query_local, (local_tokens, HEADS, 2, head_dim)).reshape(
        local_tokens, 2 * HEADS, head_dim
    )
    query_rows = lax.all_to_all(query_both, "seq", split_axis=1, concat_axis=0, tiled=True)

    def split_rows(array):
        halves = array.reshape(2, local_tokens // 2, HEADS, head_dim)
        return jnp.transpose(halves, (1, 2, 0, 3)).reshape(local_tokens // 2, 2 * HEADS, head_dim)

    new_keys, new_values = (
        lax.all_to_all(split_rows(fresh_keys), "seq", split_axis=1, concat_axis=0, tiled=True),
        lax.all_to_all(split_rows(fresh_values), "seq", split_axis=1, concat_axis=0, tiled=True),
    )
    fresh_live = jnp.ones((patch_tokens // 2,), dtype=jnp.bool_)
    key_side = jnp.mod(seq_index * rows_here + 0, 2)
    live = jnp.concatenate(
        [
            stale_mask(key_side, key_half, video_tokens, patch_start, patch_tokens, text_limit),
            fresh_live,
        ]
    )
    keys_all = jnp.concatenate([stale_keys[0, 0, 0], new_keys[:, 0]], axis=0)
    values_all = jnp.concatenate([stale_values[0, 0, 0], new_values[:, 0]], axis=0)
    summed_row, highest_row, totals_row = partial_attention(
        query_rows[:, 0], keys_all, values_all, live, scale
    )
    summed_list = [summed_row]
    highest_list = [highest_row]
    totals_list = [totals_row]
    summed = jnp.stack(summed_list, axis=1)
    highest = jnp.stack(highest_list, axis=1)
    totals = jnp.stack(totals_list, axis=1)
    back_summed, back_highest, back_totals = (
        lax.all_to_all(summed, "seq", split_axis=0, concat_axis=1, tiled=True),
        lax.all_to_all(highest, "seq", split_axis=0, concat_axis=1, tiled=True),
        lax.all_to_all(totals, "seq", split_axis=0, concat_axis=1, tiled=True),
    )
    partial_value, lse = normalize(back_summed, back_highest, back_totals)
    attended = combine_halves(
        partial_value.reshape(local_tokens, HEADS, 2, head_dim), lse.reshape(local_tokens, HEADS, 2)
    )
    attended = attended.reshape(local_tokens, features)
    gate = lax.dynamic_index_in_dim(gate_table, timestep, 0, keepdims=False)
    section_out = (hidden[0, 0].astype(jnp.float32) + gate * attended.astype(jnp.float32)).astype(
        jnp.bfloat16
    )
    arriving = passed_along(section_out, "section", 1)
    partner = partner_2(arriving, "cfg", 0)
    branch_index = lax.axis_index("cfg")
    guided_side = jnp.where(branch_index == 0, arriving, partner).astype(jnp.float32)
    plain_side = jnp.where(branch_index == 0, partner, arriving).astype(jnp.float32)
    guided = (plain_side + GUIDE * (guided_side - plain_side)).astype(jnp.bfloat16)
    handed = jnp.where(section_index == 0, guided, arriving)
    return handed.reshape(1, 1, local_tokens, features)


def solution(mesh):
    return jax.shard_map(
        body,
        mesh=mesh,
        in_specs=(
            P("cfg", "section", "seq", None),
            P("cfg", "section", "seq", None),
            P("cfg", "section", "seq", None),
            P("cfg", "section", "seq", None),
            P("cfg", "section", "seq", None, None),
            P("cfg", "section", "seq", None, None),
            P(None, "section", None),
            P(),
            P(),
            P("cfg"),
        ),
        out_specs=P("cfg", "section", "seq", None),
        check_vma=False,
    )
```

profile of v0, /device:TPU:1, one launch (start us, length us, event | category | flops | bytes accessed | tf_op | source)
XLA Modules:
  0.0 143.9 jit_solution(462632212524104086)
XLA Ops:
  0.0 0.0 copy-start
  0.0 0.0 copy-start.2
  0.0 1.0 copy.23
  1.1 0.7 copy.18
  1.8 13.5 %all-to-all-start.1 = ((bf16[16,32,128]{2,0,1:T(8,128)(2,1)}), bf16[16,32,128]{2,0,1:T(8,128)(2,1)S(1)}, u32[]{:S(2)}, u32[]{:S(2)}) async-start(bf16[16,32,128]{2,0,1:T(8,128)(2,1)} %bitcast.13), calls=%async_computation.1 | async-start | bytes 262144 | tf_op jit(solution)/shard_map/all_to_all | solution.py:106
  16.6 0.9 copy.24
  17.5 0.7 copy.19
  18.2 0.9 copy.22
  19.2 5.3 %all-to-all-done.1 = bf16[16,32,128]{2,0,1:T(8,128)(2,1)S(1)} async-done(((bf16[16,32,128]{2,0,1:T(8,128)(2,1)}), bf16[16,32,128]{2,0,1:T(8,128)(2,1)S(1)}, u32[]{:S(2)}, u32[]{:S(2)}) %all-to-all-start.1) | async-done | bytes 131104 | tf_op jit(solution)/shard_map/all_to_all | solution.py:106
  24.6 4.2 %all-to-all-start.2 = ((bf16[16,32,128]{2,0,1:T(8,128)(2,1)}), bf16[16,32,128]{2,0,1:T(8,128)(2,1)S(1)}, u32[]{:S(2)}, u32[]{:S(2)}) async-start(bf16[16,32,128]{2,0,1:T(8,128)(2,1)} %bitcast.19), calls=%async_computation.2 | async-start | bytes 262144 | tf_op jit(solution)/shard_map/all_to_all | solution.py:107
  28.8 0.0 copy-done.2
  28.9 0.1 pad_maximum_fusion
  28.9 9.3 %all-to-all-done.2 = bf16[16,32,128]{2,0,1:T(8,128)(2,1)S(1)} async-done(((bf16[16,32,128]{2,0,1:T(8,128)(2,1)}), bf16[16,32,128]{2,0,1:T(8,128)(2,1)S(1)}, u32[]{:S(2)}, u32[]{:S(2)}) %all-to-all-start.2) | async-done | bytes 131104 | tf_op jit(solution)/shard_map/all_to_all | solution.py:107
  38.2 0.7 broadcast_in_dim.42
  39.0 3.9 %all-to-all-start = ((bf16[32,32,128]{2,0,1:T(8,128)(2,1)}), bf16[32,32,128]{2,0,1:T(8,128)(2,1)S(1)}, u32[]{:S(2)}, u32[]{:S(2)}) async-start(bf16[32,32,128]{2,0,1:T(8,128)(2,1)} %bitcast.7), calls=%async_computation | async-start | bytes 524288 | tf_op jit(solution)/shard_map/all_to_all | solution.py:99
  42.8 1.3 pad_maximum_fusion.1
  44.2 8.6 %all-to-all-done = bf16[32,32,128]{2,0,1:T(8,128)(2,1)S(1)} async-done(((bf16[32,32,128]{2,0,1:T(8,128)(2,1)}), bf16[32,32,128]{2,0,1:T(8,128)(2,1)S(1)}, u32[]{:S(2)}, u32[]{:S(2)}) %all-to-all-start) | async-done | bytes 262176 | tf_op jit(solution)/shard_map/all_to_all | solution.py:99
  52.7 0.0 copy-start.3
  52.8 24.0 %while.14 = (s32[]{:T(128)}, f32[2,512,128]{2,1,0:T(8,128)}, f32[2,512]{1,0:T(2,128)S(1)}, f32[2,512]{1,0:T(2,128)S(1)}, pred[4736]{0:T(1024)(128)(4,1)S(1)}, /*...) while((s32[]{:T(128)}, f32[2,512,128]{2,1,0:T(8,128)}, ...), condition=%wide.region_3.4_spmd, body=%wide.region_0.3_spmd.sunk | while | flops 1268186112 | bytes 70744968 | solution.py:53
  52.8 1.7 %fusion.46 = (f32[512]{0:T(512)S(1)}, f32[512,4736]{1,0:T(8,128)S(1)}) fusion(pred[4736]{0:T(1024)(128)(4,1)S(1)} %get-tuple-element.149, bf16[4736,128]{1,0:T(8,128)(2,1)S(1)} %get-tuple-element.151, bf16[2,512,128]{2,1,0:T(8,128)(2,1)S(1)} %get-tuple-element.150, s32[]{:T(128)} %get-tuple-element.135), kind=kOutput, calls=%fused_computation.2.clone.1 | convolution fusion | flops 628030976 | bytes 11049988 | tf_op jit(solution)/shard_map/while/body/eval_jaxpr/dot_general | solution.py:41
  54.5 0.0 copy-start.1
  54.5 2.2 %fusion.48 = f32[512]{0:T(512)S(1)} fusion(f32[512,4736]{1,0:T(8,128)S(1)} %get-tuple-element.123, f32[512]{0:T(512)S(1)} %get-tuple-element.124, pred[4736]{0:T(1024)(128)(4,1)S(1)} %get-tuple-element.149), kind=kLoop, calls=%fused_computation.3.clone.1 | loop fusion | flops 9698816 | bytes 9708160 | tf_op jit(solution)/shard_map/while/body/eval_jaxpr/reduce_sum | solution.py:49
  56.7 1.5 %copy-done.1 = f32[512,4736]{1,0:T(8,128)} copy-done((f32[512,4736]{1,0:T(8,128)}, f32[512,4736]{1,0:T(8,128)S(1)}, u32[]{:S(2)}) %copy-start.1) | copy-done | bytes 9699352 | tf_op jit(solution)/shard_map/while
  58.3 6.5 %fusion.47 = f32[2,512,128]{2,1,0:T(8,128)} fusion(f32[2,512,128]{2,1,0:T(8,128)} %get-tuple-element.136, s32[]{:T(128)} %get-tuple-element.135, bf16[4736,128]{1,0:T(8,128)(2,1)S(1)} %get-tuple-element.152, f32[512,4736]{1,0:T(8,128)} %copy-done.1, f32[512]{0:T(512)S(1)} %get-tuple-element.124, pred[4736]{0:T(1024)(128)(4,1)S(1)} %get-tuple-element.149), kind=kOutput, calls=%fused_computation.8.clone.1 | convolution fusion | flops 630456320 | bytes 11181184 | tf_op jit(solution)/shard_map/while/body/eval_jaxpr/dot_general | solution.py:50
  64.7 1.7 %fusion.46 = (f32[512]{0:T(512)S(1)}, f32[512,4736]{1,0:T(8,128)S(1)}) fusion(pred[4736]{0:T(1024)(128)(4,1)S(1)} %get-tuple-element.149, bf16[4736,128]{1,0:T(8,128)(2,1)S(1)} %get-tuple-element.151, bf16[2,512,128]{2,1,0:T(8,128)(2,1)S(1)} %get-tuple-element.150, s32[]{:T(128)} %get-tuple-element.135), kind=kOutput, calls=%fused_computation.2.clone.1 | convolution fusion | flops 628030976 | bytes 11049988 | tf_op jit(solution)/shard_map/while/body/eval_jaxpr/dot_general | solution.py:41
  66.5 0.0 copy-start.1
  66.5 2.2 %fusion.48 = f32[512]{0:T(512)S(1)} fusion(f32[512,4736]{1,0:T(8,128)S(1)} %get-tuple-element.123, f32[512]{0:T(512)S(1)} %get-tuple-element.124, pred[4736]{0:T(1024)(128)(4,1)S(1)} %get-tuple-element.149), kind=kLoop, calls=%fused_computation.3.clone.1 | loop fusion | flops 9698816 | bytes 9708160 | tf_op jit(solution)/shard_map/while/body/eval_jaxpr/reduce_sum | solution.py:49
  68.7 1.5 %copy-done.1 = f32[512,4736]{1,0:T(8,128)} copy-done((f32[512,4736]{1,0:T(8,128)}, f32[512,4736]{1,0:T(8,128)S(1)}, u32[]{:S(2)}) %copy-start.1) | copy-done | bytes 9699352 | tf_op jit(solution)/shard_map/while
  70.3 6.5 %fusion.47 = f32[2,512,128]{2,1,0:T(8,128)} fusion(f32[2,512,128]{2,1,0:T(8,128)} %get-tuple-element.136, s32[]{:T(128)} %get-tuple-element.135, bf16[4736,128]{1,0:T(8,128)(2,1)S(1)} %get-tuple-element.152, f32[512,4736]{1,0:T(8,128)} %copy-done.1, f32[512]{0:T(512)S(1)} %get-tuple-element.124, pred[4736]{0:T(1024)(128)(4,1)S(1)} %get-tuple-element.149), kind=kOutput, calls=%fused_computation.8.clone.1 | convolution fusion | flops 630456320 | bytes 11181184 | tf_op jit(solution)/shard_map/while/body/eval_jaxpr/dot_general | solution.py:50
  76.7 0.7 all_to_all.85
  77.4 4.1 %all-to-all-start.4 = ((f32[32,32,1]{1,2,0:T(1,128)}), f32[32,32,1]{1,2,0:T(1,128)S(1)}, u32[]{:S(2)}, u32[]{:S(2)}) async-start(f32[32,32,1]{1,2,0:T(1,128)} %all_to_all.85), calls=%async_computation.4 | async-start | bytes 32768 | tf_op jit(solution)/shard_map/all_to_all | solution.py:131
  81.6 0.1 all_to_all.88
  81.7 8.8 %all-to-all-done.4 = f32[32,32,1]{1,2,0:T(1,128)S(1)} async-done(((f32[32,32,1]{1,2,0:T(1,128)}), f32[32,32,1]{1,2,0:T(1,128)S(1)}, u32[]{:S(2)}, u32[]{:S(2)}) %all-to-all-start.4) | async-done | bytes 4128 | tf_op jit(solution)/shard_map/all_to_all | solution.py:131
  90.4 11.9 %all_to_all.98 = f32[32,32,1]{1,2,0:T(1,128)S(1)} all-to-all(f32[32,32,1]{1,2,0:T(1,128)S(1)} %all_to_all.88), channel_id=1, replica_groups=mesh['section'=8,'seq'=32,'cfg'=2] {'seq'}, dimensions={0} | all-to-all | bytes 8192 | tf_op jit(solution)/shard_map/all_to_all | solution.py:130
  102.4 3.9 %all-to-all-start.3 = ((f32[1024,1,128]{2,1,0:T(1,128)}), f32[1024,1,128]{2,1,0:T(1,128)S(1)}, u32[]{:S(2)}, u32[]{:S(2)}) async-start(f32[1024,1,128]{2,1,0:T(1,128)} %bitcast.102), calls=%async_computation.3 | async-start | bytes 1048576 | tf_op jit(solution)/shard_map/all_to_all | solution.py:129
  106.9 0.0 copy-done
  106.9 0.1 fusion.34
  107.0 11.2 %all-to-all-done.3 = f32[1024,1,128]{2,1,0:T(1,128)S(1)} async-done(((f32[1024,1,128]{2,1,0:T(1,128)}), f32[1024,1,128]{2,1,0:T(1,128)S(1)}, u32[]{:S(2)}, u32[]{:S(2)}) %all-to-all-start.3) | async-done | bytes 524320 | tf_op jit(solution)/shard_map/all_to_all | solution.py:129
  118.2 0.3 multiply_reduce_fusion
  118.5 0.0 copy-done.3
  118.5 0.1 fusion.21
  118.7 7.9 %collective-permute-start = (bf16[32,2048]{1,0:T(8,128)(2,1)S(1)}, bf16[32,2048]{1,0:T(8,128)(2,1)S(1)}, u32[]{:S(2)}, u32[]{:S(2)}) collective-permute-start(bf16[32,2048]{1,0:T(8,128)(2,1)S(1)} %fusion.21), channel_id=1, source_target_pairs={{0,64},{64,128},{128,192},{192,256},{256,320},{320,384},{384,448},... | collective-permute-start | bytes 393224 | tf_op jit(solution)/shard_map/ppermute | solution.py:16
  126.6 5.8 %collective-permute-done = bf16[32,2048]{1,0:T(8,128)(2,1)S(1)} collective-permute-done((bf16[32,2048]{1,0:T(8,128)(2,1)S(1)}, bf16[32,2048]{1,0:T(8,128)(2,1)S(1)}, u32[]{:S(2)}, u32[]{:S(2)}) %collective-permute-start) | collective-permute-done | bytes 131104 | tf_op jit(solution)/shard_map/ppermute | solution.py:16
  132.4 9.8 %collective-permute-start.1 = (bf16[32,2048]{1,0:T(8,128)(2,1)S(1)}, bf16[32,2048]{1,0:T(8,128)(2,1)S(1)}, u32[]{:S(2)}, u32[]{:S(2)}) collective-permute-start(bf16[32,2048]{1,0:T(8,128)(2,1)S(1)} %collective-permute-done), channel_id=1, source_target_pairs={{0,1},{1,0},{2,3},{3,2},{4,5},{5,4},{6,7},{7,6},{8,9},{9,8},{10,11... | collective-permute-start | bytes 393224 | tf_op jit(solution)/shard_map/ppermute | solution.py:22
  142.2 1.0 collective-permute-done.1
  143.1 0.7 fusion.23
  (13 shorter events, 0.2 us)
Async XLA Ops:
  0.0 106.9 %copy-start = (f32[50,1,2048]{2,1,0:T(1,128)S(1)}, f32[50,1,2048]{2,1,0:T(1,128)}, u32[]{:S(2)}) copy-start(f32[50,1,2048]{2,1,0:T(1,128)} %param.18) | copy-start | bytes 1228804
  0.0 28.8 %copy-start.2 = (bf16[1,1,1,4224,128]{4,3,2,1,0:T(8,128)(2,1)S(1)}, bf16[1,1,1,4224,128]{4,3,2,1,0:T(8,128)(2,1)}, u32[]{:S(2)}) copy-start(bf16[1,1,1,4224,128]{4,3,2,1,0:T(8,128)(2,1)} %param.16) | copy-start | bytes 3244036
  1.8 22.8 %all-to-all-start.1 = ((bf16[16,32,128]{2,0,1:T(8,128)(2,1)}), bf16[16,32,128]{2,0,1:T(8,128)(2,1)S(1)}, u32[]{:S(2)}, u32[]{:S(2)}) async-start(bf16[16,32,128]{2,0,1:T(8,128)(2,1)} %bitcast.13), calls=%async_computation.1 | async-start | bytes 262144 | tf_op jit(solution)/shard_map/all_to_all | solution.py:106
  24.6 13.6 %all-to-all-start.2 = ((bf16[16,32,128]{2,0,1:T(8,128)(2,1)}), bf16[16,32,128]{2,0,1:T(8,128)(2,1)S(1)}, u32[]{:S(2)}, u32[]{:S(2)}) async-start(bf16[16,32,128]{2,0,1:T(8,128)(2,1)} %bitcast.19), calls=%async_computation.2 | async-start | bytes 262144 | tf_op jit(solution)/shard_map/all_to_all | solution.py:107
  39.0 13.8 %all-to-all-start = ((bf16[32,32,128]{2,0,1:T(8,128)(2,1)}), bf16[32,32,128]{2,0,1:T(8,128)(2,1)S(1)}, u32[]{:S(2)}, u32[]{:S(2)}) async-start(bf16[32,32,128]{2,0,1:T(8,128)(2,1)} %bitcast.7), calls=%async_computation | async-start | bytes 524288 | tf_op jit(solution)/shard_map/all_to_all | solution.py:99
  52.7 65.8 %copy-start.3 = (bf16[1,1,32,2048]{3,2,1,0:T(8,128)(2,1)S(1)}, bf16[1,1,32,2048]{3,2,1,0:T(8,128)(2,1)}, u32[]{:S(2)}) copy-start(bf16[1,1,32,2048]{3,2,1,0:T(8,128)(2,1)} %param.12) | copy-start | bytes 393220
  54.5 3.7 %copy-start.1 = (f32[512,4736]{1,0:T(8,128)}, f32[512,4736]{1,0:T(8,128)S(1)}, u32[]{:S(2)}) copy-start(f32[512,4736]{1,0:T(8,128)S(1)} %get-tuple-element.123) | copy-start | bytes 29097988 | tf_op jit(solution)/shard_map/while
  66.5 3.7 %copy-start.1 = (f32[512,4736]{1,0:T(8,128)}, f32[512,4736]{1,0:T(8,128)S(1)}, u32[]{:S(2)}) copy-start(f32[512,4736]{1,0:T(8,128)S(1)} %get-tuple-element.123) | copy-start | bytes 29097988 | tf_op jit(solution)/shard_map/while
  77.4 13.0 %all-to-all-start.4 = ((f32[32,32,1]{1,2,0:T(1,128)}), f32[32,32,1]{1,2,0:T(1,128)S(1)}, u32[]{:S(2)}, u32[]{:S(2)}) async-start(f32[32,32,1]{1,2,0:T(1,128)} %all_to_all.85), calls=%async_computation.4 | async-start | bytes 32768 | tf_op jit(solution)/shard_map/all_to_all | solution.py:131
  102.4 15.8 %all-to-all-start.3 = ((f32[1024,1,128]{2,1,0:T(1,128)}), f32[1024,1,128]{2,1,0:T(1,128)S(1)}, u32[]{:S(2)}, u32[]{:S(2)}) async-start(f32[1024,1,128]{2,1,0:T(1,128)} %bitcast.102), calls=%async_computation.3 | async-start | bytes 1048576 | tf_op jit(solution)/shard_map/all_to_all | solution.py:129
  118.7 13.7 %collective-permute-start = (bf16[32,2048]{1,0:T(8,128)(2,1)S(1)}, bf16[32,2048]{1,0:T(8,128)(2,1)S(1)}, u32[]{:S(2)}, u32[]{:S(2)}) collective-permute-start(bf16[32,2048]{1,0:T(8,128)(2,1)S(1)} %fusion.21), channel_id=1, source_target_pairs={{0,64},{64,128},{128,192},{192,256},{256,320},{320,384},{384,448},... | collective-permute-start | bytes 393224 | tf_op jit(solution)/shard_map/ppermute | solution.py:16
  132.4 10.7 %collective-permute-start.1 = (bf16[32,2048]{1,0:T(8,128)(2,1)S(1)}, bf16[32,2048]{1,0:T(8,128)(2,1)S(1)}, u32[]{:S(2)}, u32[]{:S(2)}) collective-permute-start(bf16[32,2048]{1,0:T(8,128)(2,1)S(1)} %collective-permute-done), channel_id=1, source_target_pairs={{0,1},{1,0},{2,3},{3,2},{4,5},{5,4},{6,7},{7,6},{8,9},{9,8},{10,11... | collective-permute-start | bytes 393224 | tf_op jit(solution)/shard_map/ppermute | solution.py:22
where the time goes:
time: 145 us; the launch traced here: 144 us
  waiting for transfers between devices  49.9 us (34%)
  starting transfers between devices  47.3 us (33%)
  matrix products  16.4 us (11%)
  blocking collectives  11.9 us (8%)
  local copies, waits for them, and re-layouts  9.07 us (6%)
  other arithmetic  7.08 us (5%)
  between operations  2.21 us (2%)
    all_to_all x1, starting transfers between devices, body(): lax.all_to_all(split_rows(fresh_keys), 'seq', split_axis=1, concat_axis=0...  13.5 us
    dot_general x2, matrix products, one_block(): jnp.dot(exps.astype(jnp.bfloat16), values_all, preferred_element_type=jnp...  12.9 us
    all_to_all x1, blocking collectives, body(): lax.all_to_all(highest, 'seq', split_axis=0, concat_axis=1, tiled=True)  11.9 us
    all_to_all x1, waiting for transfers between devices, body(): lax.all_to_all(summed, 'seq', split_axis=0, concat_axis=1, tiled=True)  11.2 us
    ppermute x1, starting transfers between devices, partner_2(): return lax.ppermute(value, axis, pairs)  9.77 us
    all_to_all x1, waiting for transfers between devices, body(): lax.all_to_all(split_rows(fresh_values), 'seq', split_axis=1, concat_axis...  9.28 us
    all_to_all x1, waiting for transfers between devices, body(): lax.all_to_all(totals, 'seq', split_axis=0, concat_axis=1, tiled=True)  8.79 us
    all_to_all x1, waiting for transfers between devices, body(): lax.all_to_all(query_both, 'seq', split_axis=1, concat_axis=0, tiled=True)  8.59 us
  transfers between devices with their start and end apart: 7, of which 7 were waited for; matrix products, arithmetic and copies ran while one was open for 3% of the time, Pallas kernels for 0%

commit v1 on v0

v1 whole, which is shorter than its diff:
```python
import functools
import math

import jax
import jax.numpy as jnp
from jax import lax
from jax.experimental import pallas as pl
from jax.experimental.pallas import tpu as pltpu
from jax.sharding import PartitionSpec as P

HEADS = 16
DIM = 128
PATCHES = 8
PATCH = 1024
VIDEO = 8192
GUIDE = 5.0
MESH = pl.DeviceIdType.MESH

N_SEQ = 32
N_SECTION = 8
TOKENS = 32
HALF = 16
STALE = 4224
FRESH = 512
KEYS = STALE + FRESH
CHUNK = 512
N_CHUNK = PATCH // CHUNK
BLOCKS = CHUNK // TOKENS
STALE_BLOCKS = (1024, 1024, 1024, 1152)
LOG2E = math.log2(math.e)
RATE = DIM**-0.5 * LOG2E


def peer_of(z, y, k):
    j = lax.rem(k, 8)
    step = lax.div(j + 1, 2)
    offset = jnp.where(lax.rem(j, 2) == 1, step, 8 - step)
    other = lax.rem(y + offset, 8)
    plane = lax.bitwise_xor(z, lax.div(k, 8))
    return plane * 8 + other


def kernel(
    patch_ref,
    text_ref,
    time_ref,
    hidden_hbm,
    q_hbm,
    k_hbm,
    v_hbm,
    sk_hbm,
    sv_hbm,
    gate_hbm,
    out_ref,
    q_in,
    k_in,
    v_in,
    h_in,
    q_out,
    kv_out,
    hid_out,
    q_all,
    kv_land,
    hid_land,
    keys,
    vals,
    gates,
    high,
    acc,
    part,
    lse_s,
    lse_out,
    part_land,
    lse_land,
    fin,
    core_out,
    core_land,
    in_sem,
    stale_sem,
    q_send,
    q_recv,
    kv_send,
    kv_recv,
    hid_send,
    hid_recv,
    part_send,
    part_recv,
    lse_send,
    lse_recv,
    core_send,
    core_recv,
    fin_send,
    fin_recv,
    okay,
):
    section = lax.axis_index("section")
    seq = lax.axis_index("seq")
    core = lax.axis_index("cfg")
    z = lax.div(seq, 8)
    y = lax.rem(seq, 8)
    head = lax.div(seq, 2)
    side = lax.rem(seq, 2)
    partner = lax.bitwise_xor(seq, 1)
    following = lax.rem(section + 1, N_SECTION)
    previous = lax.rem(section + N_SECTION - 1, N_SECTION)
    last = section == N_SECTION - 1
    head_cols = pl.ds(pl.multiple_of(head * DIM, DIM), DIM)

    barrier = pltpu.get_barrier_semaphore()

    def greet(k, carry):
        pl.semaphore_signal(
            barrier, inc=1, device_id={"seq": peer_of(z, y, k)}, device_id_type=MESH
        )
        return carry

    lax.fori_loop(1, N_SEQ, greet, 0)
    pl.semaphore_signal(barrier, inc=1, device_id={"section": following}, device_id_type=MESH)

    @pl.when(last)
    def _():
        pl.semaphore_signal(barrier, inc=1, device_id={"cfg": 1 - core}, device_id_type=MESH)

    loads = [
        pltpu.make_async_copy(src, dst, in_sem.at[i])
        for i, (src, dst) in enumerate(
            [
                (q_hbm, q_in),
                (k_hbm, k_in),
                (v_hbm, v_in),
                (hidden_hbm, h_in),
                (gate_hbm.at[:, 0, head_cols], gates),
            ]
        )
    ]
    for load in loads:
        load.start()
    stale_k = pltpu.make_async_copy(sk_hbm, keys.at[pl.ds(0, STALE)], stale_sem.at[0])
    stale_v = pltpu.make_async_copy(
        sv_hbm, vals.at[pl.ds(0, STALE), pl.ds(0, DIM)], stale_sem.at[1]
    )
    stale_k.start()
    stale_v.start()

    loads[0].wait()
    for h in range(HEADS):
        q_out[h] = q_in[:, h * DIM : (h + 1) * DIM]
    loads[1].wait()
    loads[2].wait()
    for h in range(HEADS):
        for r in range(2):
            rows = slice(r * HALF, (r + 1) * HALF)
            cols = slice(h * DIM, (h + 1) * DIM)
            kv_out[2 * h + r, 0] = k_in[rows, cols]
            kv_out[2 * h + r, 1] = v_in[rows, cols]
    loads[3].wait()
    for h in range(HEADS):
        for r in range(2):
            rows = slice(r * HALF, (r + 1) * HALF)
            cols = slice(h * DIM, (h + 1) * DIM)
            hid_out[2 * h + r] = h_in[rows, cols]

    pl.semaphore_wait(barrier, N_SEQ + jnp.where(last, 1, 0))
    pl.semaphore_signal(okay, inc=1, device_id={"section": previous}, device_id_type=MESH)

    mine = pl.ds(pl.multiple_of(seq * TOKENS, TOKENS), TOKENS)
    own_q = pltpu.make_async_copy(q_out.at[head], q_all.at[mine], q_recv.at[z])
    own_kv = pltpu.make_async_copy(kv_out.at[seq], kv_land.at[seq], kv_recv)
    own_hid = pltpu.make_async_copy(hid_out.at[seq], hid_land.at[seq], hid_recv)

    def send_q(k, carry):
        p = peer_of(z, y, k)
        pltpu.make_async_remote_copy(
            src_ref=q_out.at[lax.div(p, 2)],
            dst_ref=q_all.at[mine],
            send_sem=q_send,
            recv_sem=q_recv.at[z],
            device_id={"seq": p},
            device_id_type=MESH,
        ).start()
        return carry

    def send_kv(k, carry):
        p = peer_of(z, y, k)
        pltpu.make_async_remote_copy(
            src_ref=kv_out.at[p],
            dst_ref=kv_land.at[seq],
            send_sem=kv_send,
            recv_sem=kv_recv,
            device_id={"seq": p},
            device_id_type=MESH,
        ).start()
        return carry

    def send_hid(k, carry):
        p = peer_of(z, y, k)
        pltpu.make_async_remote_copy(
            src_ref=hid_out.at[p],
            dst_ref=hid_land.at[seq],
            send_sem=hid_send,
            recv_sem=hid_recv,
            device_id={"seq": p},
            device_id_type=MESH,
        ).start()
        return carry

    own_q.start()
    own_kv.start()
    own_hid.start()
    lax.fori_loop(1, N_SEQ, send_q, 0)
    lax.fori_loop(1, N_SEQ, send_kv, 0)
    lax.fori_loop(1, N_SEQ, send_hid, 0)

    patch_start = lax.rem(patch_ref[0] - section + PATCHES, PATCHES) * PATCH
    text_live = text_ref[0]
    first = side * STALE
    stale_k.wait()
    stale_v.wait()
    dead_first = jnp.logical_and(first >= patch_start, first < patch_start + PATCH)
    use_far = jnp.where(dead_first, 1.0, 0.0).astype(jnp.float32)
    spare = (
        keys[0:16, :].astype(jnp.float32)[0:1] * (1.0 - use_far)
        + keys[2048:2064, :].astype(jnp.float32)[0:1] * use_far
    )

    def mask_rows(i, carry):
        rows = pl.ds(pl.multiple_of(i * 128, 128), 128)
        position = first + i * 128 + lax.broadcasted_iota(jnp.int32, (128, DIM), 0)
        outside = jnp.logical_or(position < patch_start, position >= patch_start + PATCH)
        video = jnp.logical_and(position < VIDEO, outside)
        text = jnp.logical_and(position >= VIDEO, position - VIDEO < text_live)
        live = jnp.logical_or(video, text)
        key_rows = keys[rows, :].astype(jnp.float32)
        keys[rows, :] = jnp.where(live, key_rows, spare).astype(jnp.bfloat16)
        value_rows = vals[rows, 0:DIM].astype(jnp.float32)
        vals[rows, 0:DIM] = jnp.where(live, value_rows, 0.0).astype(jnp.bfloat16)
        vals[rows, DIM : 2 * DIM] = jnp.where(live, 1.0, 0.0).astype(jnp.bfloat16)
        return carry

    lax.fori_loop(0, STALE // 128, mask_rows, 0)
    vals[STALE:KEYS, DIM : 2 * DIM] = jnp.ones((FRESH, DIM), jnp.bfloat16)

    def attend(q, start, count, top, total):
        scores = lax.dot_general(
            q,
            keys[start : start + count, :],
            (((1,), (1,)), ((), ())),
            preferred_element_type=jnp.float32,
        )
        block_top = jnp.max(scores, axis=1, keepdims=True)
        new_top = block_top if top is None else jnp.maximum(top, block_top)
        weights = jnp.exp2((scores - new_top) * RATE).astype(jnp.bfloat16)
        summed = jnp.dot(
            weights, vals[start : start + count, :], preferred_element_type=jnp.float32
        )
        if top is not None:
            summed = total * jnp.exp2((top - new_top) * RATE) + summed
        return new_top, summed

    half_rows = CHUNK // 2

    def chunk_at(i):
        return lax.bitwise_xor(lax.div(z, 2), i)

    def stale_pass(i, carry):
        c = chunk_at(i)
        rows = pl.ds(pl.multiple_of(c * CHUNK, CHUNK), CHUNK)
        for g in range(2):
            plane = 2 * c + g
            plane_rows = q_all.at[pl.ds(pl.multiple_of(plane * 256, 256), 256)]
            pltpu.make_async_copy(plane_rows, plane_rows, q_recv.at[plane]).wait()
        q = q_all[rows, :]
        top, total, start = None, None, 0
        for count in STALE_BLOCKS:
            top, total = attend(q, start, count, top, total)
            start += count
        high[rows, :] = top
        acc[rows, :] = total
        return carry

    lax.fori_loop(0, N_CHUNK, stale_pass, 0)

    pltpu.make_async_copy(kv_land, kv_land, kv_recv).wait()
    keys[STALE:KEYS, :] = kv_land[:, 0].reshape(FRESH, DIM)
    vals[STALE:KEYS, 0:DIM] = kv_land[:, 1].reshape(FRESH, DIM)

    def part_copy(c):
        blocks = pl.ds(pl.multiple_of(c * BLOCKS, BLOCKS), BLOCKS)
        return pltpu.make_async_remote_copy(
            src_ref=part.at[blocks, 1 - side],
            dst_ref=part_land.at[blocks],
            send_sem=part_send.at[c],
            recv_sem=part_recv.at[c],
            device_id={"seq": partner},
            device_id_type=MESH,
        )

    def lse_copy(c):
        return pltpu.make_async_remote_copy(
            src_ref=lse_out.at[c],
            dst_ref=lse_land.at[c],
            send_sem=lse_send.at[c],
            recv_sem=lse_recv.at[c],
            device_id={"seq": partner},
            device_id_type=MESH,
        )

    def fresh_pass(i, carry):
        c = chunk_at(i)
        rows = pl.ds(pl.multiple_of(c * CHUNK, CHUNK), CHUNK)
        blocks = pl.ds(pl.multiple_of(c * BLOCKS, BLOCKS), BLOCKS)
        top, total = attend(q_all[rows, :], STALE, FRESH, high[rows, :], acc[rows, :])
        weight = total[:, DIM : 2 * DIM]
        partial = (total[:, 0:DIM] / weight).astype(jnp.bfloat16)
        part[blocks] = partial.reshape(BLOCKS, 2, HALF, DIM)
        part_copy(c).start()
        lse = top * RATE + jnp.log2(weight)
        lse_s[blocks] = lse.reshape(BLOCKS, 2, HALF, DIM)
        away = lse_s[blocks, 1 - side].reshape(half_rows, DIM)
        lse_out[c] = jnp.transpose(away)[0:8, :]
        lse_copy(c).start()
        return carry

    lax.fori_loop(0, N_CHUNK, fresh_pass, 0)

    loads[4].wait()
    gate = gates[pl.ds(time_ref[0], 1), :]
    pltpu.make_async_copy(hid_land, hid_land, hid_recv).wait()
    pl.semaphore_wait(okay, 1)

    def core_copy(c):
        blocks = pl.ds(pl.multiple_of(c * BLOCKS, BLOCKS), BLOCKS)
        return pltpu.make_async_remote_copy(
            src_ref=core_out.at[blocks],
            dst_ref=core_land.at[blocks],
            send_sem=core_send.at[c],
            recv_sem=core_recv.at[c],
            device_id={"cfg": 1 - core},
            device_id_type=MESH,
        )

    def send_fin(c):
        def send_block(b, carry):
            token_device = c * BLOCKS + b
            pltpu.make_async_remote_copy(
                src_ref=fin.at[token_device],
                dst_ref=out_ref.at[pl.ds(pl.multiple_of(side * HALF, HALF), HALF), head_cols],
                send_sem=fin_send,
                recv_sem=fin_recv,
                device_id={"section": following, "seq": token_device},
                device_id_type=MESH,
            ).start()
            return carry

        lax.fori_loop(0, BLOCKS, send_block, 0)

    def combine_pass(i, carry):
        c = chunk_at(i)
        blocks = pl.ds(pl.multiple_of(c * BLOCKS, BLOCKS), BLOCKS)
        lse_copy(c).wait_recv()
        part_copy(c).wait_recv()
        own_lse = lse_s[blocks, side].reshape(half_rows, DIM)
        other_lse = jnp.transpose(jnp.broadcast_to(lse_land[c, 0:1, :], (DIM, half_rows)))
        joint = jnp.maximum(own_lse, other_lse)
        own_weight = jnp.exp2(own_lse - joint)
        other_weight = jnp.exp2(other_lse - joint)
        own_part = part[blocks, side].reshape(half_rows, DIM).astype(jnp.float32)
        other_part = part_land[blocks].reshape(half_rows, DIM).astype(jnp.float32)
        merged = (own_part * own_weight + other_part * other_weight) / (own_weight + other_weight)
        attended = merged.astype(jnp.bfloat16).astype(jnp.float32)
        held = hid_land[blocks].reshape(half_rows, DIM).astype(jnp.float32)
        result = (held + gate * attended).astype(jnp.bfloat16).reshape(BLOCKS, HALF, DIM)

        @pl.when(last)
        def _():
            core_out[blocks] = result
            core_copy(c).start()

        @pl.when(jnp.logical_not(last))
        def _():
            fin[blocks] = result
            send_fin(c)

        return carry

    lax.fori_loop(0, N_CHUNK, combine_pass, 0)

    @pl.when(last)
    def _():
        def guide_pass(i, carry):
            c = chunk_at(i)
            blocks = pl.ds(pl.multiple_of(c * BLOCKS, BLOCKS), BLOCKS)
            core_copy(c).wait_recv()
            here = core_out[blocks].astype(jnp.float32)
            there = core_land[blocks].astype(jnp.float32)
            is_first = jnp.where(core == 0, 1.0, 0.0).astype(jnp.float32)
            guided_side = here * is_first + there * (1.0 - is_first)
            plain_side = there * is_first + here * (1.0 - is_first)
            fin[blocks] = (plain_side + GUIDE * (guided_side - plain_side)).astype(jnp.bfloat16)
            send_fin(c)
            core_copy(c).wait_send()
            return carry

        lax.fori_loop(0, N_CHUNK, guide_pass, 0)

    def drain(i, carry):
        part_copy(i).wait_send()
        lse_copy(i).wait_send()
        return carry

    lax.fori_loop(0, N_CHUNK, drain, 0)

    def sent(ref, sem):
        pltpu.make_async_copy(ref, ref, sem).wait()

    for _ in range(2):
        sent(q_out.at[pl.ds(0, 15)], q_send)
    sent(q_out.at[0], q_send)
    sent(kv_out.at[pl.ds(0, N_SEQ - 1)], kv_send)
    sent(hid_out.at[pl.ds(0, N_SEQ - 1)], hid_send)
    sent(fin, fin_send)
    pltpu.make_async_copy(fin, fin, fin_recv).wait()


def body(
    hidden, queries, fresh_keys, fresh_values, stale_keys, stale_values, gate_table, timestep,
    patch_index, text_lengths,
):
    bf16, f32 = jnp.bfloat16, jnp.float32
    flat = (TOKENS, HEADS * DIM)
    dma, regular = pltpu.SemaphoreType.DMA, pltpu.SemaphoreType.REGULAR
    scratch = [
        pltpu.VMEM(flat, bf16),
        pltpu.VMEM(flat, bf16),
        pltpu.VMEM(flat, bf16),
        pltpu.VMEM(flat, bf16),
        pltpu.VMEM((HEADS, TOKENS, DIM), bf16),
        pltpu.VMEM((N_SEQ, 2, HALF, DIM), bf16),
        pltpu.VMEM((N_SEQ, HALF, DIM), bf16),
        pltpu.VMEM((PATCH, DIM), bf16),
        pltpu.VMEM((N_SEQ, 2, HALF, DIM), bf16),
        pltpu.VMEM((N_SEQ, HALF, DIM), bf16),
        pltpu.VMEM((KEYS, DIM), bf16),
        pltpu.VMEM((KEYS, 2 * DIM), bf16),
        pltpu.VMEM((50, DIM), f32),
        pltpu.VMEM((PATCH, 1), f32),
        pltpu.VMEM((PATCH, 2 * DIM), f32),
        pltpu.VMEM((N_SEQ, 2, HALF, DIM), bf16),
        pltpu.VMEM((N_SEQ, 2, HALF, DIM), f32),
        pltpu.VMEM((N_CHUNK, 8, CHUNK // 2), f32),
        pltpu.VMEM((N_SEQ, HALF, DIM), bf16),
        pltpu.VMEM((N_CHUNK, 8, CHUNK // 2), f32),
        pltpu.VMEM((N_SEQ, HALF, DIM), bf16),
        pltpu.VMEM((N_SEQ, HALF, DIM), bf16),
        pltpu.VMEM((N_SEQ, HALF, DIM), bf16),
        dma((5,)),
        dma((2,)),
        dma,
        dma((4,)),
        dma,
        dma,
        dma,
        dma,
        dma((N_CHUNK,)),
        dma((N_CHUNK,)),
        dma((N_CHUNK,)),
        dma((N_CHUNK,)),
        dma((N_CHUNK,)),
        dma((N_CHUNK,)),
        dma,
        dma,
        regular,
    ]
    smem = pl.BlockSpec(memory_space=pltpu.SMEM)
    anywhere = pl.BlockSpec(memory_space=pl.ANY)
    out = pl.pallas_call(
        kernel,
        out_shape=jax.ShapeDtypeStruct(flat, bf16),
        in_specs=[smem] * 3 + [anywhere] * 7,
        out_specs=anywhere,
        scratch_shapes=scratch,
        compiler_params=pltpu.CompilerParams(
            collective_id=0, has_side_effects=True, vmem_limit_bytes=56 * 2**20
        ),
        cost_estimate=pl.CostEstimate(
            flops=4 * PATCH * KEYS * DIM, bytes_accessed=2**22, transcendentals=PATCH * KEYS
        ),
    )(
        patch_index.reshape(1),
        text_lengths,
        timestep.reshape(1),
        hidden.reshape(flat),
        queries.reshape(flat),
        fresh_keys.reshape(flat),
        fresh_values.reshape(flat),
        stale_keys.reshape(STALE, DIM),
        stale_values.reshape(STALE, DIM),
        gate_table,
    )
    return out.reshape(1, 1, TOKENS, HEADS * DIM)


def solution(mesh):
    rows = P("cfg", "section", "seq", None)
    stale = P("cfg", "section", "seq", None, None)
    return jax.shard_map(
        body,
        mesh=mesh,
        in_specs=(
            rows, rows, rows, rows, stale, stale, P(None, "section", None), P(), P(), P("cfg"),
        ),
        out_specs=rows,
        check_vma=False,
    )
```

time: 145 us -> 52.9 us (0.36)
  waiting for transfers between devices: 49.9 us -> 0 us
  Pallas kernels: 0 us -> 49.2 us
  starting transfers between devices: 47.3 us -> 0 us
  matrix products: 16.4 us -> 0 us
  blocking collectives: 11.9 us -> 0 us
  local copies, waits for them, and re-layouts: 9.07 us -> 1.57 us
  other arithmetic: 7.08 us -> 0 us
    pallas_call x0 -> x1, Pallas kernels: none -> 49.2 us  [body(): pl.pallas_call(kernel, out_shape=jax.ShapeDtypeStruct(flat, bf16), in_spe...]
    all_to_all x5 -> x0, waiting for transfers between devices: 43.2 us -> none  [the longest x1 11.2 us: body(): lax.all_to_all(summed, 'seq', split_axis=0, concat_axis=1, tiled=True)]
    all_to_all x5 -> x0, starting transfers between devices: 29.6 us -> none  [the longest x1 13.5 us: body(): lax.all_to_all(split_rows(fresh_keys), 'seq', split_axis=1, concat_axis=0...]
    ppermute x2 -> x0, starting transfers between devices: 17.7 us -> none  [the longest x1 9.77 us: partner_2(): return lax.ppermute(value, axis, pairs)]
    dot_general x4 -> x0, matrix products: 16.4 us -> none  [the longest x2 12.9 us: one_block(): jnp.dot(exps.astype(jnp.bfloat16), values_all, preferred_element_type=jnp...]
    all_to_all x1 -> x0, blocking collectives: 11.9 us -> none  [body(): lax.all_to_all(highest, 'seq', split_axis=0, concat_axis=1, tiled=True)]
    ppermute x2 -> x0, waiting for transfers between devices: 6.72 us -> none  [the longest x1 5.77 us: passed_along(): return lax.ppermute(value, axis, pairs)]
    reduce_sum x3 -> x0, other arithmetic: 4.72 us -> none  [the longest x2 4.39 us: one_block(): totals = jnp.sum(exps, axis=1)]
  transfers between devices with their start and end apart: 7 -> 0, of which waited for: 7 -> 0; matrix products, arithmetic and copies ran while one was open for 3% -> 0% of each run, Pallas kernels for 0% -> 0%
where the time goes in v1:
time: 52.9 us; the launch traced here: 52.7 us
  Pallas kernels  49.2 us (93%)
  between operations  1.95 us (4%)
  local copies, waits for them, and re-layouts  1.57 us (3%)
    pallas_call x1, Pallas kernels, body(): pl.pallas_call(kernel, out_shape=jax.ShapeDtypeStruct(flat, bf16), in_spe...  49.2 us
    unnamed x1, local copies, waits for them, and re-layouts  1.57 us

profile of v1, /device:TPU:1, one launch (start us, length us, event | category | flops | bytes accessed | tf_op | source)
XLA Modules:
  0.0 52.7 jit_solution(16043316685873019219)
XLA Ops:
  1.9 49.2 %shard_map.100 = bf16[32,2048]{1,0:T(8,128)(2,1)} custom-call(s32[1]{0:T(128)} %bitcast.10.patch_ref, s32[1]{0:T(128)S(6)} %copy.14.text_ref, s32[1]{0:T(128)} %bitcast.9.time_ref, bf16[32,2048]{1,0:T(8,128)(2,1)} %bitcast.14, bf16[32,2048]{1,0:T(8,128)(2,1)} %bitcast.15, bf16[32,2048]{1,0:T(8,128)(2,1)} %bitcast.16, bf16[32,2048]{1,0:T(8,128)(2,1)} %bitcast.17, ...), custom_call_target="tpu_custom_call" | custom-call | flops 2483027968 | bytes 4194304 | tf_op jit(solution)/shard_map/pallas_call | solution.py:476
  51.1 1.6 %copy.15 = bf16[1,1,32,2048]{3,2,1,0:T(8,128)(2,1)} copy(bf16[1,1,32,2048]{3,2,1,0:T(8,128)(2,1)} %bitcast.11) | data formatting | bytes 262144

commit v2 on v1

v2 whole, which is shorter than its diff:
```python
import functools
import math

import jax
import jax.numpy as jnp
from jax import lax
from jax.experimental import pallas as pl
from jax.experimental.pallas import tpu as pltpu
from jax.sharding import PartitionSpec as P

HEADS = 16
DIM = 128
PATCHES = 8
PATCH = 1024
VIDEO = 8192
GUIDE = 5.0
MESH = pl.DeviceIdType.MESH

N_SECTION = 8
TOKENS = 32
STALE = 4224
FRESH = 512
KEYS = STALE + FRESH
PLANES = 4
NEAR = 4
PLANE_ROWS = NEAR * TOKENS
ROWS = 2 * PLANE_ROWS
SIDE_ROWS = PLANES * PLANE_ROWS
STALE_PARTS = ((0, 1024), (1024, 1024), (2048, 1024), (3072, 1152))
FRESH_PART = (STALE, FRESH)
LOG2E = math.log2(math.e)
RATE = DIM**-0.5 * LOG2E


def kernel(
    patch_hbm,
    text_hbm,
    time_hbm,
    hidden_hbm,
    q_hbm,
    k_hbm,
    v_hbm,
    sk_hbm,
    sv_hbm,
    gate_hbm,
    out_ref,
    q_in,
    k_in,
    v_in,
    h_in,
    kv_out,
    q_all,
    kv_land,
    hid_land,
    keys,
    vals,
    gates,
    high,
    acc,
    part_out,
    part_own,
    part_land,
    lse_own,
    lse_out,
    lse_land,
    fin,
    core_out,
    core_land,
    patch_ref,
    text_ref,
    time_ref,
    in_sem,
    stale_sem,
    q_send,
    q_recv,
    pass_send,
    pass_recv,
    kv_send,
    kv_recv,
    hid_send,
    hid_recv,
    part_send,
    part_recv,
    lse_send,
    lse_recv,
    core_send,
    core_recv,
    fin_send,
    fin_recv,
    above,
    okay,
):
    section = lax.axis_index("section")
    seq = lax.axis_index("seq")
    core = lax.axis_index("cfg")
    z = seq >> 3
    y = seq & 7
    head = seq >> 1
    side = seq & 1
    partner = seq ^ 1
    following = (section + 1) & 7
    previous = (section + 7) & 7
    odd = (section & 1) == 1
    last = section == N_SECTION - 1

    def cols_of(h):
        return pl.ds(pl.multiple_of(h * DIM, DIM), DIM)

    barrier = pltpu.get_barrier_semaphore()
    for step in (4, 3, 5, 2, 6, 1, 7):
        pl.semaphore_signal(
            barrier, inc=1, device_id={"seq": (z << 3) | ((y + step) & 7)}, device_id_type=MESH
        )

    @pl.when(jnp.logical_not(odd))
    def _():
        for other in (following, previous):
            pl.semaphore_signal(
                barrier, inc=1, device_id={"section": other}, device_id_type=MESH
            )

    @pl.when(last)
    def _():
        pl.semaphore_signal(barrier, inc=1, device_id={"cfg": 1 - core}, device_id_type=MESH)

    loads = [
        pltpu.make_async_copy(src, dst, in_sem.at[i])
        for i, (src, dst) in enumerate(
            [
                (q_hbm, q_in),
                (k_hbm, k_in),
                (v_hbm, v_in),
                (hidden_hbm, h_in),
                (gate_hbm.at[:, 0, cols_of(head)], gates),
                (patch_hbm, patch_ref),
                (text_hbm, text_ref),
                (time_hbm, time_ref),
            ]
        )
    ]
    for load in loads:
        load.start()
    stale_k = pltpu.make_async_copy(sk_hbm, keys.at[pl.ds(0, STALE)], stale_sem.at[0])
    stale_v = pltpu.make_async_copy(
        sv_hbm, vals.at[pl.ds(0, STALE), pl.ds(0, DIM)], stale_sem.at[1]
    )
    stale_k.start()
    stale_v.start()
    for load in loads[:3]:
        load.wait()
    for h in range(HEADS):
        kv_out[h, 0] = k_in[:, h * DIM : (h + 1) * DIM]
        kv_out[h, 1] = v_in[:, h * DIM : (h + 1) * DIM]
    loads[3].wait()

    def slot_of(pair):
        return (y - pair + 3) & 7

    def nearest(plane, turn):
        pair = (plane << 3) | ((y + 2 * turn) & 6)
        slot = slot_of(pair)
        return pair | (slot >> 2), pair >> 1, slot

    def q_rows(slot):
        start = (slot >> 2) * SIDE_ROWS + z * PLANE_ROWS + (slot & 3) * TOKENS
        return pl.ds(pl.multiple_of(start, TOKENS), TOKENS)

    def block_of(slot):
        return z * NEAR + (slot & 3)

    mine = slot_of(seq & 30)
    own_q = pltpu.make_async_copy(
        q_in.at[:, cols_of(head)], q_all.at[q_rows(mine)], q_recv.at[z >> 1]
    )
    own_kv = pltpu.make_async_copy(kv_out.at[head], kv_land.at[block_of(mine)], kv_recv)
    own_hid = pltpu.make_async_copy(
        h_in.at[:, cols_of(head)], hid_land.at[block_of(mine)], hid_recv
    )
    own_q.start()
    own_kv.start()
    own_hid.start()

    def send_q(plane, turn):
        target, h, slot = nearest(plane, turn)
        pltpu.make_async_remote_copy(
            src_ref=q_in.at[:, cols_of(h)],
            dst_ref=q_all.at[q_rows(slot)],
            send_sem=q_send,
            recv_sem=q_recv.at[z >> 1],
            device_id={"seq": target},
            device_id_type=MESH,
        ).start()

    def send_kv(plane, turn):
        target, h, slot = nearest(plane, turn)
        pltpu.make_async_remote_copy(
            src_ref=kv_out.at[h],
            dst_ref=kv_land.at[block_of(slot)],
            send_sem=kv_send,
            recv_sem=kv_recv,
            device_id={"seq": target},
            device_id_type=MESH,
        ).start()

    def send_hid(plane, turn):
        target, h, slot = nearest(plane, turn)
        pltpu.make_async_remote_copy(
            src_ref=h_in.at[:, cols_of(h)],
            dst_ref=hid_land.at[block_of(slot)],
            send_sem=hid_send,
            recv_sem=hid_recv,
            device_id={"seq": target},
            device_id_type=MESH,
        ).start()

    own_plane, all_planes = (2, 1, 3), (2, 1, 3, 0)

    pl.semaphore_wait(
        barrier,
        7 + jnp.where(z > 0, 1, 0) + jnp.where(odd, 2, 0) + jnp.where(last, 1, 0),
    )

    @pl.when(z < PLANES - 1)
    def _():
        pl.semaphore_signal(barrier, inc=1, device_id={"seq": seq + 8}, device_id_type=MESH)

    for down in (3, 2, 1):

        @pl.when(z >= down)
        def _():
            pl.semaphore_signal(
                above.at[z], inc=1, device_id={"seq": seq - 8 * down}, device_id_type=MESH
            )

    for turn in own_plane:
        send_q(z, turn)
    for apart in (1, 2, 3):
        plane = z ^ apart

        @pl.when(plane > z)
        def _():
            pl.semaphore_wait(above.at[plane], 1)

        for turn in all_planes:
            send_q(plane, turn)

    @pl.when(odd)
    def _():
        for other in (following, previous):
            pl.semaphore_signal(okay, inc=1, device_id={"section": other}, device_id_type=MESH)

    for apart in (3, 2, 1):
        for turn in all_planes:
            send_kv(z ^ apart, turn)
    for turn in own_plane:
        send_kv(z, turn)
    for apart in (3, 2, 1):
        for turn in all_planes:
            send_hid(z ^ apart, turn)
    for turn in own_plane:
        send_hid(z, turn)

    for load in loads[4:]:
        load.wait()
    patch_start = lax.rem(patch_ref[0] - section + PATCHES, PATCHES) * PATCH
    text_live = text_ref[0]
    first = side * STALE
    stale_k.wait()
    stale_v.wait()
    dead_first = jnp.logical_and(first >= patch_start, first < patch_start + PATCH)
    use_far = jnp.where(dead_first, 1.0, 0.0).astype(jnp.float32)
    spare = (
        keys[0:16, :].astype(jnp.float32)[0:1] * (1.0 - use_far)
        + keys[2048:2064, :].astype(jnp.float32)[0:1] * use_far
    )

    def mask_rows(i, carry):
        rows = pl.ds(pl.multiple_of(i * 128, 128), 128)
        position = first + i * 128 + lax.broadcasted_iota(jnp.int32, (128, DIM), 0)
        outside = jnp.logical_or(position < patch_start, position >= patch_start + PATCH)
        video = jnp.logical_and(position < VIDEO, outside)
        text = jnp.logical_and(position >= VIDEO, position - VIDEO < text_live)
        live = jnp.logical_or(video, text)
        key_rows = keys[rows, :].astype(jnp.float32)
        keys[rows, :] = jnp.where(live, key_rows, spare).astype(jnp.bfloat16)
        value_rows = vals[rows, 0:DIM].astype(jnp.float32)
        vals[rows, 0:DIM] = jnp.where(live, value_rows, 0.0).astype(jnp.bfloat16)
        vals[rows, DIM : 2 * DIM] = jnp.where(live, 1.0, 0.0).astype(jnp.bfloat16)
        return carry

    lax.fori_loop(0, STALE // 128, mask_rows, 0)
    vals[STALE:KEYS, DIM : 2 * DIM] = jnp.ones((FRESH, DIM), jnp.bfloat16)

    def attend(rows, parts, resume):
        q = q_all[rows, :]
        top = high[rows, :] if resume else None
        total = acc[rows, :] if resume else None

        def scores_of(part):
            start, count = part
            return lax.dot_general(
                q,
                keys[start : start + count, :],
                (((1,), (1,)), ((), ())),
                preferred_element_type=jnp.float32,
            )

        ahead = scores_of(parts[0])
        for n, (start, count) in enumerate(parts):
            scores = ahead
            if n + 1 < len(parts):
                ahead = scores_of(parts[n + 1])
            part_top = jnp.max(scores, axis=1, keepdims=True)
            new_top = part_top if top is None else jnp.maximum(top, part_top)
            weights = jnp.exp2((scores - new_top) * RATE).astype(jnp.bfloat16)
            summed = jnp.dot(
                weights, vals[start : start + count, :], preferred_element_type=jnp.float32
            )
            if top is not None:
                summed = total * jnp.exp2((top - new_top) * RATE) + summed
            top, total = new_top, summed
        return top, total

    def keep(rows, state):
        high[rows, :], acc[rows, :] = state

    def finished(state):
        top, total = state
        weight = total[:, DIM : 2 * DIM]
        partial = (total[:, 0:DIM] / weight).astype(jnp.bfloat16)
        return partial, top * RATE + jnp.log2(weight)

    near_base, far_base = side * SIDE_ROWS, (1 - side) * SIDE_ROWS

    def chunk_rows(base, planes):
        return pl.ds(pl.multiple_of(base + planes * ROWS, ROWS), ROWS)

    def wait_bytes(ref, sem):
        pltpu.make_async_copy(ref, ref, sem).wait()

    def pass_copy(planes):
        rows = q_all.at[chunk_rows(near_base, planes)]
        return pltpu.make_async_remote_copy(
            src_ref=rows,
            dst_ref=rows,
            send_sem=pass_send.at[planes],
            recv_sem=pass_recv.at[planes],
            device_id={"seq": partner},
            device_id_type=MESH,
        )

    def part_copy(planes):
        return pltpu.make_async_remote_copy(
            src_ref=part_out.at[planes],
            dst_ref=part_land.at[planes],
            send_sem=part_send.at[planes],
            recv_sem=part_recv.at[planes],
            device_id={"seq": partner},
            device_id_type=MESH,
        )

    def lse_copy(planes):
        return pltpu.make_async_remote_copy(
            src_ref=lse_out.at[planes],
            dst_ref=lse_land.at[planes],
            send_sem=lse_send.at[planes],
            recv_sem=lse_recv.at[planes],
            device_id={"seq": partner},
            device_id_type=MESH,
        )

    def core_copy(planes):
        return pltpu.make_async_remote_copy(
            src_ref=core_out.at[planes],
            dst_ref=core_land.at[planes],
            send_sem=core_send.at[planes],
            recv_sem=core_recv.at[planes],
            device_id={"cfg": 1 - core},
            device_id_type=MESH,
        )

    def send_fin(planes):
        for b in range(2 * NEAR):
            plane = 2 * planes + b // NEAR
            token_y = ((seq & 6) + 4 * side + b % NEAR + 5) & 7
            pltpu.make_async_remote_copy(
                src_ref=fin.at[planes, pl.ds(b * TOKENS, TOKENS)],
                dst_ref=out_ref.at[:, cols_of(head)],
                send_sem=fin_send,
                recv_sem=fin_recv,
                device_id={"section": following, "seq": (plane << 3) | token_y},
                device_id_type=MESH,
            ).start()

    def guide(planes):
        core_copy(planes).wait_recv()
        here = core_out[planes].astype(jnp.float32)
        there = core_land[planes].astype(jnp.float32)
        is_first = core == 0
        guided_side = jnp.where(is_first, here, there)
        plain_side = jnp.where(is_first, there, here)
        fin[planes] = (plain_side + GUIDE * (guided_side - plain_side)).astype(jnp.bfloat16)
        send_fin(planes)

    def combine(planes):
        lse_copy(planes).wait_recv()
        part_copy(planes).wait_recv()
        lse_here = lse_own[planes]
        lse_there = jnp.transpose(jnp.broadcast_to(lse_land[planes, 0:1, :], (DIM, ROWS)))
        joint = jnp.maximum(lse_here, lse_there)
        weight_here = jnp.exp2(lse_here - joint)
        weight_there = jnp.exp2(lse_there - joint)
        merged = part_own[planes].astype(jnp.float32) * weight_here
        merged += part_land[planes].astype(jnp.float32) * weight_there
        attended = (merged / (weight_here + weight_there)).astype(jnp.bfloat16)
        held = hid_land[pl.ds(planes * 2 * NEAR, 2 * NEAR)].reshape(ROWS, DIM)
        result = held.astype(jnp.float32) + gate * attended.astype(jnp.float32)
        result = result.astype(jnp.bfloat16)

        @pl.when(last)
        def _():
            core_out[planes] = result
            core_copy(planes).start()

        @pl.when(jnp.logical_not(last))
        def _():
            fin[planes] = result
            send_fin(planes)

    def send_part(planes, state):
        partial, lse = finished(state)
        part_out[planes] = partial
        part_copy(planes).start()
        lse_out[planes] = jnp.transpose(lse)[0:8, :]
        lse_copy(planes).start()

    def keep_part(planes, state):
        part_own[planes], lse_own[planes] = finished(state)

    def pass_on(planes):
        wait_bytes(q_all.at[chunk_rows(near_base, planes)], q_recv.at[planes])
        pass_copy(planes).start()

    one, two = z >> 1, (z >> 1) ^ 1
    near_one, near_two = chunk_rows(near_base, one), chunk_rows(near_base, two)
    far_one, far_two = chunk_rows(far_base, one), chunk_rows(far_base, two)

    pass_on(one)
    keep(near_one, attend(near_one, STALE_PARTS, False))
    pass_on(two)

    @pl.when(jnp.logical_not(odd))
    def _():
        pl.semaphore_wait(okay, 2)
        for other in (following, previous):
            pl.semaphore_signal(okay, inc=1, device_id={"section": other}, device_id_type=MESH)

    wait_bytes(q_all.at[far_one], pass_recv.at[one])
    keep(far_one, attend(far_one, STALE_PARTS, False))

    wait_bytes(kv_land, kv_recv)
    keys[STALE:KEYS, :] = kv_land[:, 0].reshape(FRESH, DIM)
    vals[STALE:KEYS, 0:DIM] = kv_land[:, 1].reshape(FRESH, DIM)
    send_part(one, attend(far_one, (FRESH_PART,), True))
    keep_part(one, attend(near_one, (FRESH_PART,), True))
    wait_bytes(q_all.at[far_two], pass_recv.at[two])
    send_part(two, attend(far_two, STALE_PARTS + (FRESH_PART,), False))

    @pl.when(odd)
    def _():
        pl.semaphore_wait(okay, 2)

    gate = gates[pl.ds(time_ref[0], 1), :]
    wait_bytes(hid_land, hid_recv)
    combine(one)
    keep(near_two, attend(near_two, STALE_PARTS[:2], False))

    @pl.when(last)
    def _():
        guide(one)

    keep_part(two, attend(near_two, STALE_PARTS[2:] + (FRESH_PART,), True))
    combine(two)

    @pl.when(last)
    def _():
        guide(two)
        for planes in range(2):
            core_copy(planes).wait_send()

    for planes in range(2):
        pass_copy(planes).wait_send()
        part_copy(planes).wait_send()
        lse_copy(planes).wait_send()
    rest = HEADS - 1
    wait_bytes(q_all.at[pl.ds(0, rest * TOKENS)], q_send)
    wait_bytes(kv_out.at[pl.ds(0, rest)], kv_send)
    wait_bytes(hid_land.at[pl.ds(0, rest)], hid_send)
    wait_bytes(fin, fin_send)
    wait_bytes(fin, fin_recv)


def body(
    hidden, queries, fresh_keys, fresh_values, stale_keys, stale_values, gate_table, timestep,
    patch_index, text_lengths,
):
    bf16, f32 = jnp.bfloat16, jnp.float32
    flat = (TOKENS, HEADS * DIM)
    dma, regular = pltpu.SemaphoreType.DMA, pltpu.SemaphoreType.REGULAR
    scratch = [
        pltpu.VMEM(flat, bf16),
        pltpu.VMEM(flat, bf16),
        pltpu.VMEM(flat, bf16),
        pltpu.VMEM(flat, bf16),
        pltpu.VMEM((HEADS, 2, TOKENS, DIM), bf16),
        pltpu.VMEM((PATCH, DIM), bf16),
        pltpu.VMEM((HEADS, 2, TOKENS, DIM), bf16),
        pltpu.VMEM((HEADS, TOKENS, DIM), bf16),
        pltpu.VMEM((KEYS, DIM), bf16),
        pltpu.VMEM((KEYS, 2 * DIM), bf16),
        pltpu.VMEM((50, DIM), f32),
        pltpu.VMEM((PATCH, 1), f32),
        pltpu.VMEM((PATCH, 2 * DIM), f32),
        pltpu.VMEM((2, ROWS, DIM), bf16),
        pltpu.VMEM((2, ROWS, DIM), bf16),
        pltpu.VMEM((2, ROWS, DIM), bf16),
        pltpu.VMEM((2, ROWS, DIM), f32),
        pltpu.VMEM((2, 8, ROWS), f32),
        pltpu.VMEM((2, 8, ROWS), f32),
        pltpu.VMEM((2, ROWS, DIM), bf16),
        pltpu.VMEM((2, ROWS, DIM), bf16),
        pltpu.VMEM((2, ROWS, DIM), bf16),
        pltpu.SMEM((1,), jnp.int32),
        pltpu.SMEM((1,), jnp.int32),
        pltpu.SMEM((1,), jnp.int32),
        dma((8,)),
        dma((2,)),
        dma,
        dma((2,)),
        dma((2,)),
        dma((2,)),
        dma,
        dma,
        dma,
        dma,
        dma((2,)),
        dma((2,)),
        dma((2,)),
        dma((2,)),
        dma((2,)),
        dma((2,)),
        dma,
        dma,
        regular((PLANES,)),
        regular,
    ]
    anywhere = pl.BlockSpec(memory_space=pl.ANY)
    out = pl.pallas_call(
        kernel,
        out_shape=pltpu.VMEM(flat, bf16),
        in_specs=[anywhere] * 10,
        out_specs=pl.BlockSpec(memory_space=pltpu.VMEM),
        scratch_shapes=scratch,
        compiler_params=pltpu.CompilerParams(
            collective_id=0, has_side_effects=True, vmem_limit_bytes=56 * 2**20
        ),
        cost_estimate=pl.CostEstimate(
            flops=4 * PATCH * KEYS * DIM, bytes_accessed=2**22, transcendentals=PATCH * KEYS
        ),
    )(
        patch_index.reshape(1),
        text_lengths,
        timestep.reshape(1),
        hidden.reshape(flat),
        queries.reshape(flat),
        fresh_keys.reshape(flat),
        fresh_values.reshape(flat),
        stale_keys.reshape(STALE, DIM),
        stale_values.reshape(STALE, DIM),
        gate_table,
    )
    return out.reshape(1, 1, TOKENS, HEADS * DIM)


def solution(mesh):
    rows = P("cfg", "section", "seq", None)
    stale = P("cfg", "section", "seq", None, None)
    return jax.shard_map(
        body,
        mesh=mesh,
        in_specs=(
            rows, rows, rows, rows, stale, stale, P(None, "section", None), P(), P(), P("cfg"),
        ),
        out_specs=rows,
        check_vma=False,
    )
```

time: 52.9 us -> 47.6 us (0.90)
  Pallas kernels: 49.2 us -> 44.8 us
  local copies, waits for them, and re-layouts: 1.57 us -> 0.66 us
    pallas_call x1, Pallas kernels: 49.2 us -> 44.8 us  [body(): pl.pallas_call(kernel, out_shape=pltpu.VMEM(flat, bf16), in_specs=[anywhe...]
    unnamed x1, local copies, waits for them, and re-layouts: 1.57 us -> 0.66 us
where the time goes in v2:
time: 47.6 us; the launch traced here: 47.4 us
  Pallas kernels  44.8 us (94%)
  between operations  1.95 us (4%)
  local copies, waits for them, and re-layouts  0.66 us (1%)
    pallas_call x1, Pallas kernels, body(): pl.pallas_call(kernel, out_shape=pltpu.VMEM(flat, bf16), in_specs=[anywhe...  44.8 us

profile of v2, /device:TPU:1, one launch (start us, length us, event | category | flops | bytes accessed | tf_op | source)
XLA Modules:
  0.0 47.4 jit_solution(16228629180658799243)
XLA Ops:
  1.9 44.8 %shard_map.100 = bf16[32,2048]{1,0:T(8,128)(2,1)S(1)} custom-call(s32[1]{0:T(128)} %bitcast.10.patch_hbm, s32[1]{0:T(128)S(6)} %copy.15.text_hbm, s32[1]{0:T(128)} %bitcast.9.time_hbm, bf16[32,2048]{1,0:T(8,128)(2,1)} %bitcast.14, bf16[32,2048]{1,0:T(8,128)(2,1)} %bitcast.15, bf16[32,2048]{1,0:T(8,128)(2,1)} %bitcast.16, bf16[32,2048]{1,0:T(8,128)(2,1)} %bitcast.17, ...), custom_call_target="tpu_custom_call" | custom-call | flops 2483027968 | bytes 4194304 | tf_op jit(solution)/shard_map/pallas_call | solution.py:558
  46.8 0.7 %copy.12 = bf16[1,1,32,2048]{3,2,1,0:T(8,128)(2,1)} copy(bf16[1,1,32,2048]{3,2,1,0:T(8,128)(2,1)S(1)} %bitcast.11) | data formatting | bytes 262144

commit v3 on v2

--- a/solution.py
+++ b/solution.py
@@ -64,7 +64,6 @@
     lse_out,
     lse_land,
     fin,
-    core_out,
     core_land,
     patch_ref,
     text_ref,
@@ -101,7 +100,7 @@
     following = (section + 1) & 7
     previous = (section + 7) & 7
     odd = (section & 1) == 1
-    last = section == N_SECTION - 1
+    first_section = section == 0
 
     def cols_of(h):
         return pl.ds(pl.multiple_of(h * DIM, DIM), DIM)
@@ -119,7 +118,7 @@
                 barrier, inc=1, device_id={"section": other}, device_id_type=MESH
             )
 
-    @pl.when(last)
+    @pl.when(first_section)
     def _():
         pl.semaphore_signal(barrier, inc=1, device_id={"cfg": 1 - core}, device_id_type=MESH)
 
@@ -146,12 +145,6 @@
     )
     stale_k.start()
     stale_v.start()
-    for load in loads[:3]:
-        load.wait()
-    for h in range(HEADS):
-        kv_out[h, 0] = k_in[:, h * DIM : (h + 1) * DIM]
-        kv_out[h, 1] = v_in[:, h * DIM : (h + 1) * DIM]
-    loads[3].wait()
 
     def slot_of(pair):
         return (y - pair + 3) & 7
@@ -174,11 +167,8 @@
     )
     own_kv = pltpu.make_async_copy(kv_out.at[head], kv_land.at[block_of(mine)], kv_recv)
     own_hid = pltpu.make_async_copy(
-        h_in.at[:, cols_of(head)], hid_land.at[block_of(mine)], hid_recv
-    )
-    own_q.start()
-    own_kv.start()
-    own_hid.start()
+        h_in.at[:, cols_of(head)], hid_land.at[block_of(mine)], hid_recv.at[z >> 1]
+    )
 
     def send_q(plane, turn):
         target, h, slot = nearest(plane, turn)
@@ -208,7 +198,7 @@
             src_ref=h_in.at[:, cols_of(h)],
             dst_ref=hid_land.at[block_of(slot)],
             send_sem=hid_send,
-            recv_sem=hid_recv,
+            recv_sem=hid_recv.at[z >> 1],
             device_id={"seq": target},
             device_id_type=MESH,
         ).start()
@@ -217,7 +207,7 @@
 
     pl.semaphore_wait(
         barrier,
-        7 + jnp.where(z > 0, 1, 0) + jnp.where(odd, 2, 0) + jnp.where(last, 1, 0),
+        7 + jnp.where(z > 0, 1, 0) + jnp.where(odd, 2, 0) + jnp.where(first_section, 1, 0),
     )
 
     @pl.when(z < PLANES - 1)
@@ -232,34 +222,59 @@
                 above.at[z], inc=1, device_id={"seq": seq - 8 * down}, device_id_type=MESH
             )
 
-    for turn in own_plane:
-        send_q(z, turn)
-    for apart in (1, 2, 3):
-        plane = z ^ apart
-
+    def hear(plane):
         @pl.when(plane > z)
         def _():
             pl.semaphore_wait(above.at[plane], 1)
 
+    def send_to(send, plane):
         for turn in all_planes:
-            send_q(plane, turn)
-
-    @pl.when(odd)
-    def _():
-        for other in (following, previous):
-            pl.semaphore_signal(okay, inc=1, device_id={"section": other}, device_id_type=MESH)
-
-    for apart in (3, 2, 1):
+            send(plane, turn)
+
+    def lay_out():
+        loads[1].wait()
+        loads[2].wait()
+        for h in range(HEADS):
+            kv_out[h, 0] = k_in[:, h * DIM : (h + 1) * DIM]
+            kv_out[h, 1] = v_in[:, h * DIM : (h + 1) * DIM]
+        own_kv.start()
+
+    def start_q():
+        loads[0].wait()
+        own_q.start()
+
+    def send_own(send):
+        for turn in own_plane:
+            send(z, turn)
+
+    def greet_back():
+        @pl.when(odd)
+        def _():
+            for other in (following, previous):
+                pl.semaphore_signal(
+                    okay, inc=1, device_id={"section": other}, device_id_type=MESH
+                )
+
+    def send_all_hid():
+        loads[3].wait()
+        own_hid.start()
         for turn in all_planes:
-            send_kv(z ^ apart, turn)
-    for turn in own_plane:
-        send_kv(z, turn)
-    for apart in (3, 2, 1):
-        for turn in all_planes:
-            send_hid(z ^ apart, turn)
-    for turn in own_plane:
-        send_hid(z, turn)
-
+            for apart in (3, 0, 2, 1):
+                if apart or turn:
+                    send_hid(z ^ apart, turn)
+
+    start_q()
+    send_own(send_q)
+    for n in range(PLANES - 1):
+        plane = n + jnp.where(z <= n, 1, 0)
+        hear(plane)
+        send_to(send_q, plane)
+    greet_back()
+    lay_out()
+    for turn in all_planes:
+        for apart in (3, 0, 2, 1):
+            if apart or turn:
+                send_kv(z ^ apart, turn)
     for load in loads[4:]:
         load.wait()
     patch_start = lax.rem(patch_ref[0] - section + PATCHES, PATCHES) * PATCH
@@ -369,38 +384,22 @@
             device_id_type=MESH,
         )
 
-    def core_copy(planes):
-        return pltpu.make_async_remote_copy(
-            src_ref=core_out.at[planes],
-            dst_ref=core_land.at[planes],
-            send_sem=core_send.at[planes],
-            recv_sem=core_recv.at[planes],
-            device_id={"cfg": 1 - core},
-            device_id_type=MESH,
-        )
-
     def send_fin(planes):
+        first_y = ((seq & 6) + 4 * side + 5) & 7
+        turned = jnp.where(first_y == 5, 3, 0)
         for b in range(2 * NEAR):
             plane = 2 * planes + b // NEAR
-            token_y = ((seq & 6) + 4 * side + b % NEAR + 5) & 7
+            place = (b % NEAR) ^ turned
+            token_y = (first_y + place) & 7
+            start = (b // NEAR) * NEAR * TOKENS + place * TOKENS
             pltpu.make_async_remote_copy(
-                src_ref=fin.at[planes, pl.ds(b * TOKENS, TOKENS)],
+                src_ref=fin.at[planes, pl.ds(pl.multiple_of(start, TOKENS), TOKENS)],
                 dst_ref=out_ref.at[:, cols_of(head)],
                 send_sem=fin_send,
                 recv_sem=fin_recv,
                 device_id={"section": following, "seq": (plane << 3) | token_y},
                 device_id_type=MESH,
             ).start()
-
-    def guide(planes):
-        core_copy(planes).wait_recv()
-        here = core_out[planes].astype(jnp.float32)
-        there = core_land[planes].astype(jnp.float32)
-        is_first = core == 0
-        guided_side = jnp.where(is_first, here, there)
-        plain_side = jnp.where(is_first, there, here)
-        fin[planes] = (plain_side + GUIDE * (guided_side - plain_side)).astype(jnp.bfloat16)
-        send_fin(planes)
 
     def combine(planes):
         lse_copy(planes).wait_recv()
@@ -413,19 +412,14 @@
         merged = part_own[planes].astype(jnp.float32) * weight_here
         merged += part_land[planes].astype(jnp.float32) * weight_there
         attended = (merged / (weight_here + weight_there)).astype(jnp.bfloat16)
-        held = hid_land[pl.ds(planes * 2 * NEAR, 2 * NEAR)].reshape(ROWS, DIM)
+        blocks = pl.ds(planes * 2 * NEAR, 2 * NEAR)
+        wait_bytes(hid_land.at[blocks], hid_recv.at[planes])
+        held = hid_land[blocks].reshape(ROWS, DIM)
         result = held.astype(jnp.float32) + gate * attended.astype(jnp.float32)
         result = result.astype(jnp.bfloat16)
 
-        @pl.when(last)
-        def _():
-            core_out[planes] = result
-            core_copy(planes).start()
-
-        @pl.when(jnp.logical_not(last))
-        def _():
-            fin[planes] = result
-            send_fin(planes)
+        fin[planes] = result
+        send_fin(planes)
 
     def send_part(planes, state):
         partial, lse = finished(state)
@@ -441,7 +435,7 @@
         wait_bytes(q_all.at[chunk_rows(near_base, planes)], q_recv.at[planes])
         pass_copy(planes).start()
 
-    one, two = z >> 1, (z >> 1) ^ 1
+    one, two = 0, 1
     near_one, near_two = chunk_rows(near_base, one), chunk_rows(near_base, two)
     far_one, far_two = chunk_rows(far_base, one), chunk_rows(far_base, two)
 
@@ -462,6 +456,8 @@
     keys[STALE:KEYS, :] = kv_land[:, 0].reshape(FRESH, DIM)
     vals[STALE:KEYS, 0:DIM] = kv_land[:, 1].reshape(FRESH, DIM)
     send_part(one, attend(far_one, (FRESH_PART,), True))
+
+    send_all_hid()
     keep_part(one, attend(near_one, (FRESH_PART,), True))
     wait_bytes(q_all.at[far_two], pass_recv.at[two])
     send_part(two, attend(far_two, STALE_PARTS + (FRESH_PART,), False))
@@ -471,22 +467,10 @@
         pl.semaphore_wait(okay, 2)
 
     gate = gates[pl.ds(time_ref[0], 1), :]
-    wait_bytes(hid_land, hid_recv)
     combine(one)
-    keep(near_two, attend(near_two, STALE_PARTS[:2], False))
-
-    @pl.when(last)
-    def _():
-        guide(one)
-
-    keep_part(two, attend(near_two, STALE_PARTS[2:] + (FRESH_PART,), True))
+
+    keep_part(two, attend(near_two, STALE_PARTS + (FRESH_PART,), False))
     combine(two)
-
-    @pl.when(last)
-    def _():
-        guide(two)
-        for planes in range(2):
-            core_copy(planes).wait_send()
 
     for planes in range(2):
         pass_copy(planes).wait_send()
@@ -498,6 +482,25 @@
     wait_bytes(hid_land.at[pl.ds(0, rest)], hid_send)
     wait_bytes(fin, fin_send)
     wait_bytes(fin, fin_recv)
+
+    @pl.when(first_section)
+    def _():
+        swap = pltpu.make_async_remote_copy(
+            src_ref=out_ref,
+            dst_ref=core_land,
+            send_sem=core_send,
+            recv_sem=core_recv,
+            device_id={"cfg": 1 - core},
+            device_id_type=MESH,
+        )
+        swap.start()
+        swap.wait()
+        here = out_ref[...].astype(jnp.float32)
+        there = core_land[...].astype(jnp.float32)
+        is_first = core == 0
+        guided_side = jnp.where(is_first, here, there)
+        plain_side = jnp.where(is_first, there, here)
+        out_ref[...] = (plain_side + GUIDE * (guided_side - plain_side)).astype(jnp.bfloat16)
 
 
 def body(
@@ -528,8 +531,7 @@
         pltpu.VMEM((2, 8, ROWS), f32),
         pltpu.VMEM((2, 8, ROWS), f32),
         pltpu.VMEM((2, ROWS, DIM), bf16),
-        pltpu.VMEM((2, ROWS, DIM), bf16),
-        pltpu.VMEM((2, ROWS, DIM), bf16),
+        pltpu.VMEM(flat, bf16),
         pltpu.SMEM((1,), jnp.int32),
         pltpu.SMEM((1,), jnp.int32),
         pltpu.SMEM((1,), jnp.int32),
@@ -542,13 +544,13 @@
         dma,
         dma,
         dma,
-        dma,
-        dma((2,)),
-        dma((2,)),
-        dma((2,)),
-        dma((2,)),
-        dma((2,)),
-        dma((2,)),
+        dma((2,)),
+        dma((2,)),
+        dma((2,)),
+        dma((2,)),
+        dma((2,)),
+        dma,
+        dma,
         dma,
         dma,
         regular((PLANES,)),

time: 47.6 us -> 47.3 us (level)
  Pallas kernels: 44.8 us -> 44 us
    pallas_call x1, Pallas kernels: 44.8 us -> 44 us  [body(): pl.pallas_call(kernel, out_shape=pltpu.VMEM(flat, bf16), in_specs=[anywhe...]
where the time goes in v3:
time: 47.3 us; the launch traced here: 46.6 us
  Pallas kernels  44 us (93%)
  between operations  1.95 us (4%)
  local copies, waits for them, and re-layouts  0.66 us (1%)
    pallas_call x1, Pallas kernels, body(): pl.pallas_call(kernel, out_shape=pltpu.VMEM(flat, bf16), in_specs=[anywhe...  44 us

profile of v3, /device:TPU:1, one launch (start us, length us, event | category | flops | bytes accessed | tf_op | source)
XLA Modules:
  0.0 46.6 jit_solution(8271502597497923768)
XLA Ops:
  1.9 44.0 %shard_map.100 = bf16[32,2048]{1,0:T(8,128)(2,1)S(1)} custom-call(s32[1]{0:T(128)} %bitcast.10.patch_hbm, s32[1]{0:T(128)S(6)} %copy.15.text_hbm, s32[1]{0:T(128)} %bitcast.9.time_hbm, bf16[32,2048]{1,0:T(8,128)(2,1)} %bitcast.14, bf16[32,2048]{1,0:T(8,128)(2,1)} %bitcast.15, bf16[32,2048]{1,0:T(8,128)(2,1)} %bitcast.16, bf16[32,2048]{1,0:T(8,128)(2,1)} %bitcast.17, ...), custom_call_target="tpu_custom_call" | custom-call | flops 2483027968 | bytes 4194304 | tf_op jit(solution)/shard_map/pallas_call | solution.py:560
  46.0 0.7 %copy.12 = bf16[1,1,32,2048]{3,2,1,0:T(8,128)(2,1)} copy(bf16[1,1,32,2048]{3,2,1,0:T(8,128)(2,1)S(1)} %bitcast.11) | data formatting | bytes 262144

commit v4 on v3

--- a/solution.py
+++ b/solution.py
@@ -396,7 +396,7 @@
                 src_ref=fin.at[planes, pl.ds(pl.multiple_of(start, TOKENS), TOKENS)],
                 dst_ref=out_ref.at[:, cols_of(head)],
                 send_sem=fin_send,
-                recv_sem=fin_recv,
+                recv_sem=fin_recv.at[z],
                 device_id={"section": following, "seq": (plane << 3) | token_y},
                 device_id_type=MESH,
             ).start()
@@ -480,27 +480,39 @@
     wait_bytes(q_all.at[pl.ds(0, rest * TOKENS)], q_send)
     wait_bytes(kv_out.at[pl.ds(0, rest)], kv_send)
     wait_bytes(hid_land.at[pl.ds(0, rest)], hid_send)
-    wait_bytes(fin, fin_send)
-    wait_bytes(fin, fin_recv)
-
-    @pl.when(first_section)
-    def _():
-        swap = pltpu.make_async_remote_copy(
-            src_ref=out_ref,
-            dst_ref=core_land,
-            send_sem=core_send,
-            recv_sem=core_recv,
+    def heads_of(plane):
+        return (slice(None), pl.ds(plane * NEAR * DIM, NEAR * DIM))
+
+    def swap(plane):
+        return pltpu.make_async_remote_copy(
+            src_ref=out_ref.at[heads_of(plane)],
+            dst_ref=core_land.at[heads_of(plane)],
+            send_sem=core_send.at[plane],
+            recv_sem=core_recv.at[plane],
             device_id={"cfg": 1 - core},
             device_id_type=MESH,
         )
-        swap.start()
-        swap.wait()
-        here = out_ref[...].astype(jnp.float32)
-        there = core_land[...].astype(jnp.float32)
-        is_first = core == 0
-        guided_side = jnp.where(is_first, here, there)
-        plain_side = jnp.where(is_first, there, here)
-        out_ref[...] = (plain_side + GUIDE * (guided_side - plain_side)).astype(jnp.bfloat16)
+
+    for plane in range(PLANES):
+        wait_bytes(out_ref.at[heads_of(plane)], fin_recv.at[plane])
+
+        @pl.when(first_section)
+        def _():
+            swap(plane).start()
+
+    @pl.when(first_section)
+    def _():
+        for plane in range(PLANES):
+            swap(plane).wait()
+            here = out_ref[heads_of(plane)].astype(jnp.float32)
+            there = core_land[heads_of(plane)].astype(jnp.float32)
+            is_first = core == 0
+            guided_side = jnp.where(is_first, here, there)
+            plain_side = jnp.where(is_first, there, here)
+            guided = plain_side + GUIDE * (guided_side - plain_side)
+            out_ref[heads_of(plane)] = guided.astype(jnp.bfloat16)
+
+    wait_bytes(fin, fin_send)
 
 
 def body(
@@ -549,10 +561,10 @@
         dma((2,)),
         dma((2,)),
         dma((2,)),
+        dma((PLANES,)),
+        dma((PLANES,)),
         dma,
-        dma,
-        dma,
-        dma,
+        dma((PLANES,)),
         regular((PLANES,)),
         regular,
     ]

time: 47.3 us -> 47.2 us (level)
  no operation moved by 1% of the time
where the time goes in v4:
time: 47.2 us; the launch traced here: 46.7 us
  Pallas kernels  44.1 us (93%)
  between operations  1.95 us (4%)
  local copies, waits for them, and re-layouts  0.66 us (1%)
    pallas_call x1, Pallas kernels, body(): pl.pallas_call(kernel, out_shape=pltpu.VMEM(flat, bf16), in_specs=[anywhe...  44.1 us

profile of v4, /device:TPU:1, one launch (start us, length us, event | category | flops | bytes accessed | tf_op | source)
XLA Modules:
  0.0 46.7 jit_solution(1693098521889269740)
XLA Ops:
  1.9 44.1 %shard_map.100 = bf16[32,2048]{1,0:T(8,128)(2,1)S(1)} custom-call(s32[1]{0:T(128)} %bitcast.10.patch_hbm, s32[1]{0:T(128)S(6)} %copy.15.text_hbm, s32[1]{0:T(128)} %bitcast.9.time_hbm, bf16[32,2048]{1,0:T(8,128)(2,1)} %bitcast.14, bf16[32,2048]{1,0:T(8,128)(2,1)} %bitcast.15, bf16[32,2048]{1,0:T(8,128)(2,1)} %bitcast.16, bf16[32,2048]{1,0:T(8,128)(2,1)} %bitcast.17, ...), custom_call_target="tpu_custom_call" | custom-call | flops 2483027968 | bytes 4194304 | tf_op jit(solution)/shard_map/pallas_call | solution.py:572
  46.0 0.7 %copy.12 = bf16[1,1,32,2048]{3,2,1,0:T(8,128)(2,1)} copy(bf16[1,1,32,2048]{3,2,1,0:T(8,128)(2,1)S(1)} %bitcast.11) | data formatting | bytes 262144
